TPU v7x, 256 devices: a whole 4x4x8 slice. The times are simulated.
256 devices in a mesh: blk: 16 (over z, x_lo), fsdp: 16 (over x_hi, y, core).
Axes of the slice: x: 4 (x_hi: 2, x_lo: 2; x = x_hi * 2 + x_lo), y: 4, z: 8, core: 2. Of those that a mesh axis runs over, the one named last changes fastest.
Arguments:
- hidden: bfloat16 [32768, 6912], P(('blk', 'fsdp')), may hold values from -6 to 6
- residual: bfloat16 [16, 2560, 2048], P('blk', 'fsdp'), may hold values from -6 to 6
- cotangent: bfloat16 [16, 2560, 2048], P('blk', 'fsdp'), may hold values from -6 to 6
- weight: bfloat16 [16, 2560, 6912], P('blk', 'fsdp'), may hold values from -6 to 6
- self_sketch: float32 [16, 2560, 512], P('blk', 'fsdp'), may hold values from -6 to 6
- mix_sketch: float32 [16, 2560, 512], P('blk', 'fsdp'), may hold values from -6 to 6
- bucket: int32 [6912], replicated, may hold values from 0 to 511
- sign_bit: int32 [6912], replicated, may hold values from 0 to 1
Outputs:
- stream_out: bfloat16 [16, 2560, 2048], P('blk', 'fsdp')
- new_weight: bfloat16 [16, 2560, 6912], P('blk', 'fsdp')
- new_self: float32 [16, 2560, 512], P('blk', 'fsdp')
- new_mix: float32 [16, 2560, 512], P('blk', 'fsdp')
All inputs are finite; a program needn't handle non-finite values.
Results may differ from a plain program's by a relative error of at most 0.007.
Values may be sent and summed in bfloat16 or wider, within the bound.
A program may use at most 256 MiB of HBM per device.

v0:
```python
import jax
import jax.numpy as jnp
from jax import lax
from jax.sharding import PartitionSpec as P

step_size = 0.3
consensus_rate = 0.5


def from_behind(shard, axis, by):
    devices = lax.axis_size(axis)
    return lax.ppermute(shard, axis, [(i, (i + by) % devices) for i in range(devices)])


def expand(sketch_rows, bucket, sign_values):
    return jnp.take(sketch_rows, bucket, axis=-1) * sign_values


def compress(values, table_half, sketch_ratio):
    upper_part = values.astype(jnp.bfloat16)
    rest_one = values - lax.optimization_barrier(upper_part).astype(jnp.float32)
    middle_part = rest_one.astype(jnp.bfloat16)
    rest_two = rest_one - lax.optimization_barrier(middle_part).astype(jnp.float32)
    lower_part = rest_two.astype(jnp.bfloat16)
    total = jnp.dot(upper_part, table_half, preferred_element_type=jnp.float32)
    total = total + jnp.dot(middle_part, table_half, preferred_element_type=jnp.float32)
    total = total + jnp.dot(lower_part, table_half, preferred_element_type=jnp.float32)
    return sketch_ratio * total


def body(hidden, residual, cotangent, weight, self_sketch, mix_sketch, bucket, sign_bit):
    resid_local = residual[0]
    cotan_local = cotangent[0]
    weight_local = weight[0]
    own_sketch = self_sketch[0]
    neighbour_mix = mix_sketch[0]
    width_ff = weight_local.shape[1]
    sketch_count = own_sketch.shape[1]
    out_scale = width_ff ** (-0.5)
    sketch_ratio = sketch_count / width_ff
    sign_values = (2 * sign_bit - 1).astype(jnp.float32)
    table_half = (
        (bucket[:, None] == jnp.arange(sketch_count, dtype=jnp.int32)[None, :]).astype(jnp.float32)
        * sign_values[:, None]
    ).astype(jnp.bfloat16)
    public = expand(own_sketch, bucket, sign_values)
    weight_float = weight_local.astype(jnp.float32)
    shard_rows = lax.all_gather(hidden, "fsdp", axis=0, tiled=True)
    product = lax.dot_general(
        weight_local, shard_rows, (((1,), (1,)), ((), ())), preferred_element_type=jnp.float32
    )
    grad_total = jnp.dot(cotan_local, shard_rows, preferred_element_type=jnp.float32)
    stream_out = (resid_local.astype(jnp.float32) + out_scale * product).astype(jnp.bfloat16)
    gradient = out_scale * grad_total
    stepped = weight_float - step_size * gradient
    sketched = compress(stepped - public, table_half, sketch_ratio)
    from_left = from_behind(sketched.astype(jnp.bfloat16), "blk", 1).astype(sketched.dtype)
    from_right = from_behind(sketched.astype(jnp.bfloat16), "blk", -1).astype(sketched.dtype)
    new_self = own_sketch + sketched
    new_mix = neighbour_mix + (from_left + sketched + from_right) / 3.0
    new_weight = (
        stepped + consensus_rate * expand(new_mix - new_self, bucket, sign_values)
    ).astype(jnp.bfloat16)
    return (stream_out[None], new_weight[None], new_self[None], new_mix[None])


def solution(mesh):
    return jax.shard_map(
        body,
        mesh=mesh,
        in_specs=(
            P(("blk", "fsdp"), None),
            P("blk", "fsdp", None),
            P("blk", "fsdp", None),
            P("blk", "fsdp", None),
            P("blk", "fsdp", None),
            P("blk", "fsdp", None),
            P(),
            P(),
        ),
        out_specs=(
            P("blk", "fsdp", None),
            P("blk", "fsdp", None),
            P("blk", "fsdp", None),
            P("blk", "fsdp", None),
        ),
        check_vma=False,
    )
```

profile of v0, /device:TPU:1, one launch (start us, length us, event | category | flops | bytes accessed | tf_op | source)
XLA Modules:
  0.0 268.7 jit_solution(8359075355716164075)
XLA Ops:
  7.2 0.0 copy-start
  7.2 0.0 all-gather.2.cloned.1.call-start
  7.2 0.7 all-gather.2.cloned.1.call-update
  7.9 1.2 copy.12
  9.1 0.8 compare_select_fusion
  9.9 17.2 %gather_fusion = f32[6912,160]{1,0:T(8,128)} fusion(f32[160,512]{0,1:T(8,128)S(1)} %copy.12, s32[7168]{0:T(1024)S(1)} %pad_clamp_fusion), kind=kCustom, calls=%fused_computation.clone | custom fusion | bytes 8875008 | tf_op jit(solution)/shard_map/jit(_take)/gather | solution.py:16
  27.0 0.0 copy-start.4
  27.0 0.0 copy-start.5
  27.0 7.1 %copy.13 = f32[6912,160]{0,1:T(8,128)} copy(f32[6912,160]{1,0:T(8,128)} %gather_fusion) | data formatting | bytes 8847360 | tf_op jit(solution)/shard_map/jit(_take)/gather | solution.py:16
  34.1 0.0 copy-done.4
  34.1 0.0 copy-done.5
  34.1 148.0 %all-gather.2.cloned.1.call-done = bf16[2048,6912]{1,0:T(8,128)(2,1)} async-done(((bf16[128,6912]{1,0:T(8,128)(2,1)}), bf16[2048,6912]{1,0:T(8,128)(2,1)}) %all-gather.2.cloned.1.call-update) | async-done | bytes 28311568 | tf_op jit(solution)/shard_map/all_gather | solution.py:48
  182.1 0.0 copy-done
  182.1 19.5 %fusion.31 = (bf16[160,6912]{1,0:T(8,128)(2,1)S(1)}, f32[160,6912]{1,0:T(8,128)}, f32[160,6912]{1,0:T(8,128)}) fusion(f32[6912]{0:T(1024)S(1)} %add_convert_fusion, f32[6912,160]{0,1:T(8,128)} %copy.13, pred[6912]{0:T(1024)(128)(4,1)S(1)} %compare_and_fusion, bf16[2048,6912]{1,0:T(8,128)(2,1)} %all-gather.2.cloned.1.call-done, ...), kind=kOutput, calls=%fused_computation.48 | convolution fusion | flops 4537589760 | bytes 46696192 | tf_op jit(solution)/shard_map/dot_general | solution.py:52
  201.6 0.0 slice-start
  201.6 2.7 fusion.17
  204.3 0.0 slice-start.1
  204.3 2.5 fusion.1
  206.9 0.0 slice-done
  206.9 0.0 slice-done.1
  206.9 2.6 fusion
  209.5 2.6 fusion.33
  212.1 0.0 copy-start.2
  212.1 0.0 copy-start.3
  212.1 3.3 %collective-permute-start.1 = (bf16[160,512]{1,0:T(8,128)(2,1)S(1)}, bf16[160,512]{1,0:T(8,128)(2,1)S(1)}, u32[]{:S(2)}, u32[]{:S(2)}) collective-permute-start(bf16[160,512]{1,0:T(8,128)(2,1)S(1)} %get-tuple-element.11), channel_id=1, source_target_pairs={{0,240},{16,0},{32,16},{48,32},{64,48},{80,64},{96,80},{112,96},{1... | collective-permute-start | bytes 491528 | tf_op jit(solution)/shard_map/ppermute | solution.py:12
  215.4 0.0 collective-permute-start
  215.4 15.9 %fusion.20 = bf16[1,160,2048]{2,1,0:T(8,128)(2,1)} fusion(bf16[2048,6912]{1,0:T(8,128)(2,1)} %all-gather.2.cloned.1.call-done, bf16[1,160,6912]{2,1,0:T(8,128)(2,1)} %param.13, bf16[1,160,2048]{2,1,0:T(8,128)(2,1)} %param.11), kind=kOutput, calls=%fused_computation.30 | convolution fusion | flops 4531159040 | bytes 31834112 | tf_op jit(solution)/shard_map/dot_general | solution.py:49
  231.3 0.0 collective-permute-done.1
  231.3 0.0 collective-permute-done
  231.3 0.0 copy-done.2
  231.3 0.0 copy-done.3
  231.3 1.0 fusion.27
  232.3 0.2 copy.14
  232.5 17.2 %gather_fusion.1 = f32[6912,160]{1,0:T(8,128)} fusion(f32[160,512]{0,1:T(8,128)S(1)} %copy.14, s32[7168]{0:T(1024)S(1)} %pad_clamp_fusion), kind=kCustom, calls=%fused_computation.1.clone | custom fusion | bytes 8875008 | tf_op jit(solution)/shard_map/jit(_take)/gather | solution.py:16
  249.8 6.4 %copy.15 = f32[6912,160]{0,1:T(8,128)} copy(f32[6912,160]{1,0:T(8,128)} %gather_fusion.1) | data formatting | bytes 8847360 | tf_op jit(solution)/shard_map/jit(_take)/gather | solution.py:16
  256.2 0.0 copy-start.1
  256.2 5.7 %fusion.21 = bf16[1,160,6912]{2,1,0:T(8,128)(2,1)} fusion(f32[160,6912]{1,0:T(8,128)} %get-tuple-element.10, f32[6912,160]{0,1:T(8,128)} %copy.15, f32[6912]{0:T(1024)S(1)} %add_convert_fusion, pred[6912]{0:T(1024)(128)(4,1)S(1)} %compare_and_fusion), kind=kLoop, calls=%fused_computation.31 | loop fusion | flops 5529600 | bytes 11093760 | tf_op jit(solution)/shard_map/broadcast_in_dim | solution.py:64
  261.9 0.0 copy-done.1
  (4 shorter events, 0.0 us)
Async XLA Ops:
  7.2 174.9 %copy-start = (bf16[1,160,2048]{2,1,0:T(8,128)(2,1)S(1)}, bf16[1,160,2048]{2,1,0:T(8,128)(2,1)}, u32[]{:S(2)}) copy-start(bf16[1,160,2048]{2,1,0:T(8,128)(2,1)} %param.12) | copy-start | bytes 1966084
  7.2 174.9 %all-gather.2.cloned.1.call-start = ((), (), s32[]{:S(2)}) async-start(), calls=%async_computation | async-start | bytes 30081024 | tf_op jit(solution)/shard_map/all_gather | solution.py:48
  27.0 7.1 %copy-start.4 = (s32[6912]{0:T(1024)S(1)}, s32[6912]{0:T(1024)}, u32[]{:S(2)}) copy-start(s32[6912]{0:T(1024)} %param.16) | copy-start | bytes 82948
  27.0 7.1 %copy-start.5 = (s32[6912]{0:T(1024)S(1)}, s32[6912]{0:T(1024)}, u32[]{:S(2)}) copy-start(s32[6912]{0:T(1024)} %param.17) | copy-start | bytes 82948
  201.6 5.3 %slice-start = ((s8[4423680]{0:T(1024)(128)(4,1)}), s8[229376]{0:T(1024)(128)(4,1)S(1)}, s32[]{:S(2)}) async-start(s8[4423680]{0:T(1024)(128)(4,1)} %bitcast.48), calls=%async_computation.1 | async-start | bytes 458752
  204.3 2.6 slice-start.1
  212.1 19.2 %copy-start.2 = (f32[1,160,512]{2,1,0:T(8,128)S(1)}, f32[1,160,512]{2,1,0:T(8,128)}, u32[]{:S(2)}) copy-start(f32[1,160,512]{2,1,0:T(8,128)} %param.14) | copy-start | bytes 983044
  212.1 19.2 %copy-start.3 = (f32[1,160,512]{2,1,0:T(8,128)S(1)}, f32[1,160,512]{2,1,0:T(8,128)}, u32[]{:S(2)}) copy-start(f32[1,160,512]{2,1,0:T(8,128)} %param.15) | copy-start | bytes 983044
  212.1 19.2 %collective-permute-start.1 = (bf16[160,512]{1,0:T(8,128)(2,1)S(1)}, bf16[160,512]{1,0:T(8,128)(2,1)S(1)}, u32[]{:S(2)}, u32[]{:S(2)}) collective-permute-start(bf16[160,512]{1,0:T(8,128)(2,1)S(1)} %get-tuple-element.11), channel_id=1, source_target_pairs={{0,240},{16,0},{32,16},{48,32},{64,48},{80,64},{96,80},{112,96},{1... | collective-permute-start | bytes 491528 | tf_op jit(solution)/shard_map/ppermute | solution.py:12
  215.4 15.9 %collective-permute-start = (bf16[160,512]{1,0:T(8,128)(2,1)S(1)}, bf16[160,512]{1,0:T(8,128)(2,1)S(1)}, u32[]{:S(2)}, u32[]{:S(2)}) collective-permute-start(bf16[160,512]{1,0:T(8,128)(2,1)S(1)} %get-tuple-element.11), channel_id=1, source_target_pairs={{0,16},{16,32},{32,48},{48,64},{64,80},{80,96},{96,112},{112,128},... | collective-permute-start | bytes 491528 | tf_op jit(solution)/shard_map/ppermute | solution.py:12
  256.2 5.7 %copy-start.1 = (bf16[1,160,2048]{2,1,0:T(8,128)(2,1)S(1)}, bf16[1,160,2048]{2,1,0:T(8,128)(2,1)}, u32[]{:S(2)}) copy-start(bf16[1,160,2048]{2,1,0:T(8,128)(2,1)} %param.12) | copy-start | bytes 1966084
Sparse Core Ops, SparseCore 0:
  10.8 171.2 all-gather.1
where the time goes:
time: 269 us
  waiting for transfers between devices  149 us (55%)
  local copies, waits for them, and re-layouts  49.3 us (18%)
  matrix products  43.1 us (16%)
  between operations  14.2 us (5%)
  other arithmetic  10.1 us (4%)
  starting transfers between devices  3.34 us (1%)
    all_gather x1, waiting for transfers between devices, body(): shard_rows = lax.all_gather(hidden, 'fsdp', axis=0, tiled=True)  148 us
    gather x4, local copies, waits for them, and re-layouts, expand(): return jnp.take(sketch_rows, bucket, axis=-1) * sign_values  47.9 us
    dot_general x1, matrix products, body(): jnp.dot(cotan_local, shard_rows, preferred_element_type=jnp.float32)  19.5 us
    dot_general x1, matrix products, body(): lax.dot_general(weight_local, shard_rows, (((1,), (1,)), ((), ())), prefe...  15.9 us
    broadcast_in_dim x2, other arithmetic, body(): return (stream_out[None], new_weight[None], new_self[None], new_mix[None])  6.67 us
  transfers between devices with their start and end apart: 3, of which 1 were waited for; matrix products, arithmetic and copies ran while one was open for 16% of the time, Pallas kernels for 0%

commit v1 on v0

v1 whole, which is shorter than its diff:
```python
import functools

import jax
import jax.numpy as jnp
from jax import lax
from jax.experimental import pallas as pl
from jax.experimental.pallas import tpu as pltpu
from jax.sharding import PartitionSpec as P

MESH = pl.DeviceIdType.MESH
STEP_SIZE = 0.3
CONSENSUS = 0.5
CH = 256
LEAD = 4


def nt(a, b):
    return lax.dot_general(a, b, (((1,), (1,)), ((), ())), preferred_element_type=jnp.float32)


def nn(a, b):
    return jnp.dot(a, b, preferred_element_type=jnp.float32)


def kernel(
    hid, res, cot, wgt, slf, mix, bkt, sgn,
    out_s, out_w, out_self, out_mix,
    buf, wv, cv, rv, sv, mv, sacc, stepped, tbl, lhs, kacc, sk_send, sk_left, sk_right,
    lsem, insem, sem1, sem2, sem3, sibsem, ssem, xsem, osem,
):
    rows, ff = wgt.shape
    toks = hid.shape[0]
    nc = ff // CH
    nb, nf = lax.axis_size("blk"), lax.axis_size("fsdp")
    sk = slf.shape[1]
    blk, me = lax.axis_index("blk"), lax.axis_index("fsdp")
    xh, y, core = me // 8, (me // 2) % 4, me % 2
    xo = 1 - xh

    def at(a, b):
        return a * 8 + (b % 4) * 2 + core

    sibling = me + 1 - 2 * core
    up, down, across = at(xh, y + 1), at(xh, y + 3), at(xo, y)
    ahead, behind = (blk + 1) % nb, (blk + nb - 1) % nb

    def block(j, b):
        return buf.at[j, pl.ds(pl.multiple_of(b * toks, toks), toks), :]

    def columns(ref, j):
        return ref.at[:, pl.ds(pl.multiple_of(j * CH, CH), CH)]

    def load(j):
        return pltpu.make_async_copy(columns(hid, j), block(j, me), lsem.at[j])

    def send(j, b, to, recv, lane):
        pltpu.make_async_remote_copy(
            src_ref=block(j, b), dst_ref=block(j, b), send_sem=ssem.at[lane], recv_sem=recv.at[j],
            device_id=(blk, to), device_id_type=MESH,
        ).start()

    def arrived(j, sem, blocks):
        ref = buf.at[j, pl.ds(0, blocks * toks), :]
        pltpu.make_async_copy(ref, ref, sem.at[j]).wait()

    def own(j):
        load(j).wait()
        send(j, me, up, sem1, 0)
        send(j, me, down, sem1, 0)
        send(j, me, across, sem1, 0)
        send(j, me, sibling, sibsem, 1)

    def second(j):
        arrived(j, sem1, 3)
        kind = (j % 3) // 2
        turn = 1 + 2 * (j % 2)
        send(j, at(xh, y + 4 - turn), at(xh, y + turn), sem2, 0)
        send(j, (1 - kind) * across + kind * up, (1 - kind) * up + kind * across, sem2, 0)
        send(j, (1 - kind) * across + kind * down, (1 - kind) * down + kind * across, sem2, 0)
        send(j, up, sibling, sibsem, 1)
        send(j, down, sibling, sibsem, 1)
        send(j, across, sibling, sibsem, 1)

    def third(j):
        arrived(j, sem2, 3)
        kind = (j % 3) // 2
        turn = 1 + 2 * (1 - j % 2)
        send(
            j,
            (1 - kind) * at(xh, y + 2) + kind * at(xo, y + 4 - turn),
            (1 - kind) * across + kind * at(xh, y + turn),
            sem3,
            0,
        )
        send(j, at(xh, y + 2), sibling, sibsem, 1)
        send(j, at(xo, y + 1), sibling, sibsem, 1)
        send(j, at(xo, y + 3), sibling, sibsem, 1)

    def fourth(j):
        arrived(j, sem3, 1)
        send(j, at(xo, y + 2), sibling, sibsem, 1)

    def compute(j):
        arrived(j, sibsem, nf // 2)
        h = buf[j]
        cols = pl.ds(pl.multiple_of(j * CH, CH), CH)
        w = wv[:, cols]
        sacc[...] += nt(w, h)
        new = w.astype(jnp.float32) - (STEP_SIZE * ff**-0.5) * nn(cv[...], h)
        stepped[j] = new
        sign = (2 * sgn[:, cols] - 1).astype(jnp.float32)
        hot = lax.broadcasted_iota(jnp.int32, (sk, CH), 0) == bkt[:, cols]
        table = jnp.where(hot, jnp.broadcast_to(sign, (sk, CH)), 0.0).astype(jnp.bfloat16)
        tbl[j] = table
        high = new.astype(jnp.bfloat16)
        lhs[pl.ds(0, rows), :] = high
        lhs[pl.ds(rows, rows), :] = (new - high.astype(jnp.float32)).astype(jnp.bfloat16)
        lhs[pl.ds(2 * rows, 16), :] = jnp.broadcast_to(sign, (16, CH)).astype(jnp.bfloat16)
        kacc[...] += nt(lhs[...], table)

    for j in range(nc):
        load(j).start()
    ins = [(cot, cv), (wgt, wv), (res, rv), (slf, sv), (mix, mv)]
    ins = [pltpu.make_async_copy(a, b, insem.at[i]) for i, (a, b) in enumerate(ins)]
    for c in ins:
        c.start()
    barrier = pltpu.get_barrier_semaphore()
    for to in (up, down, across, sibling):
        pl.semaphore_signal(barrier, inc=1, device_id=(blk, to), device_id_type=MESH)
    for to in (ahead, behind):
        pl.semaphore_signal(barrier, inc=1, device_id=(to, me), device_id_type=MESH)
    pl.semaphore_wait(barrier, 6)

    def lead(j, c):
        own(j)
        return c

    lax.fori_loop(0, LEAD, lead, 0)
    sacc[...] = jnp.zeros_like(sacc)
    kacc[...] = jnp.zeros_like(kacc)
    for c in ins:
        c.wait()

    def step(i, c):
        @pl.when(i + LEAD < nc)
        def _():
            own(i + LEAD)

        @pl.when(i < nc)
        def _():
            second(i)

        @pl.when((i >= 1) & (i < nc + 1))
        def _():
            third(i - 1)

        @pl.when((i >= 2) & (i < nc + 2))
        def _():
            fourth(i - 2)

        @pl.when(i >= 3)
        def _():
            compute(i - 3)

        return c

    lax.fori_loop(0, nc + 3, step, 0)

    sketched = (sk / ff) * (
        kacc[pl.ds(0, rows), :] + kacc[pl.ds(rows, rows), :] - kacc[pl.ds(2 * rows, 1), :] * sv[...]
    )
    sk_send[...] = sketched.astype(jnp.bfloat16)
    swaps = [
        pltpu.make_async_remote_copy(
            src_ref=sk_send, dst_ref=dst, send_sem=xsem.at[2 * i], recv_sem=xsem.at[2 * i + 1],
            device_id=(to, me), device_id_type=MESH,
        )
        for i, (dst, to) in enumerate(((sk_left, ahead), (sk_right, behind)))
    ]
    for c in swaps:
        c.start()
    rv[...] = (rv[...].astype(jnp.float32) + (ff**-0.5) * sacc[...]).astype(jnp.bfloat16)
    outs = [pltpu.make_async_copy(rv, out_s, osem.at[0])]
    outs[0].start()
    sv[...] = sv[...] + sketched
    outs.append(pltpu.make_async_copy(sv, out_self, osem.at[1]))
    outs[1].start()
    mv[...] = mv[...] + sketched / 3.0
    for c in swaps:
        c.wait()
    mixed = mv[...] + (sk_left[...].astype(jnp.float32) + sk_right[...].astype(jnp.float32)) / 3.0
    mv[...] = mixed
    outs.append(pltpu.make_async_copy(mv, out_mix, osem.at[2]))
    outs[2].start()
    sk_send[...] = (CONSENSUS * (mixed - sv[...])).astype(jnp.bfloat16)

    def last(j, c):
        cols = pl.ds(pl.multiple_of(j * CH, CH), CH)
        wv[:, cols] = (stepped[j] + nn(sk_send[...], tbl[j])).astype(jnp.bfloat16)
        pltpu.make_async_copy(columns(wv, j), columns(out_w, j), osem.at[3]).start()
        return c

    lax.fori_loop(0, nc, last, 0)
    outs.append(pltpu.make_async_copy(wv, out_w, osem.at[3]))
    for c in outs:
        c.wait()
    for lane, blocks in ((0, 7), (1, 8)):
        ref = buf.at[:, pl.ds(0, blocks * toks), :]
        pltpu.make_async_copy(ref, ref, ssem.at[lane]).wait()


def body(hidden, residual, cotangent, weight, self_sketch, mix_sketch, bucket, sign_bit):
    toks, ff = hidden.shape
    _, rows, whole = residual.shape
    sk = self_sketch.shape[2]
    nc = ff // CH
    f32, bf16 = jnp.float32, jnp.bfloat16
    anywhere = pl.BlockSpec(memory_space=pl.ANY)
    vmem = pl.BlockSpec(memory_space=pltpu.VMEM)
    dma = pltpu.SemaphoreType.DMA
    outs = pl.pallas_call(
        kernel,
        out_shape=(
            jax.ShapeDtypeStruct((rows, whole), bf16),
            jax.ShapeDtypeStruct((rows, ff), bf16),
            jax.ShapeDtypeStruct((rows, sk), f32),
            jax.ShapeDtypeStruct((rows, sk), f32),
        ),
        in_specs=[anywhere] * 6 + [vmem] * 2,
        out_specs=(anywhere,) * 4,
        scratch_shapes=[
            pltpu.VMEM((nc, whole, CH), bf16),
            pltpu.VMEM((rows, ff), bf16),
            pltpu.VMEM((rows, whole), bf16),
            pltpu.VMEM((rows, whole), bf16),
            pltpu.VMEM((rows, sk), f32),
            pltpu.VMEM((rows, sk), f32),
            pltpu.VMEM((rows, whole), f32),
            pltpu.VMEM((nc, rows, CH), f32),
            pltpu.VMEM((nc, sk, CH), bf16),
            pltpu.VMEM((2 * rows + 16, CH), bf16),
            pltpu.VMEM((2 * rows + 16, sk), f32),
            pltpu.VMEM((rows, sk), bf16),
            pltpu.VMEM((rows, sk), bf16),
            pltpu.VMEM((rows, sk), bf16),
            dma((nc,)), dma((5,)), dma((nc,)), dma((nc,)), dma((nc,)), dma((nc,)), dma((2,)), dma((4,)), dma((4,)),
        ],
        compiler_params=pltpu.CompilerParams(
            collective_id=0, has_side_effects=True, vmem_limit_bytes=60 * 2**20
        ),
        cost_estimate=pl.CostEstimate(
            flops=2 * rows * ff * (2 * whole + 3 * sk), bytes_accessed=2 * (toks + 2 * rows) * ff, transcendentals=0
        ),
        name="gather_step_sketch",
    )(hidden, residual[0], cotangent[0], weight[0], self_sketch[0], mix_sketch[0], bucket[None], sign_bit[None])
    return tuple(o[None] for o in outs)


def solution(mesh):
    split = P("blk", "fsdp", None)
    return jax.shard_map(
        body,
        mesh=mesh,
        in_specs=(P(("blk", "fsdp"), None), split, split, split, split, split, P(), P()),
        out_specs=(split, split, split, split),
        check_vma=False,
    )
```

time: 269 us -> 153 us (0.57)
  waiting for transfers between devices: 149 us -> 0 us
  Pallas kernels: 0 us -> 142 us
  matrix products: 43.1 us -> 0 us
  local copies, waits for them, and re-layouts: 49.3 us -> 9.38 us
  between operations: 14.2 us -> 0.64 us
  other arithmetic: 10.1 us -> 0 us
  starting transfers between devices: 3.34 us -> 0 us
    all_gather x1 -> x0, waiting for transfers between devices: 148 us -> none  [body(): shard_rows = lax.all_gather(hidden, 'fsdp', axis=0, tiled=True)]
    pallas_call x0 -> x1, Pallas kernels: none -> 142 us  [body(): pl.pallas_call(kernel, out_shape=(jax.ShapeDtypeStruct((rows, whole), bf1...]
    gather x4 -> x0, local copies, waits for them, and re-layouts: 47.9 us -> none  [expand(): return jnp.take(sketch_rows, bucket, axis=-1) * sign_values]
    dot_general x5 -> x0, matrix products: 43.1 us -> none  [the longest x1 19.5 us: body(): jnp.dot(cotan_local, shard_rows, preferred_element_type=jnp.float32)]
    broadcast_in_dim x2 -> x0, other arithmetic: 6.67 us -> none  [body(): return (stream_out[None], new_weight[None], new_self[None], new_mix[None])]
    unnamed x16 -> x8, local copies, waits for them, and re-layouts: 0.04 us -> 6.63 us
    ppermute x2 -> x0, starting transfers between devices: 3.3 us -> none  [from_behind(): lax.ppermute(shard, axis, [(i, (i + by) % devices) for i in range(devices)])]
    broadcast_in_dim x0 -> x2, local copies, waits for them, and re-layouts: none -> 2.75 us  [the longest x1 1.38 us: body(): bucket[None]]
  transfers between devices with their start and end apart: 3 -> 0, of which waited for: 1 -> 0; matrix products, arithmetic and copies ran while one was open for 16% -> 0% of each run, Pallas kernels for 0% -> 0%
where the time goes in v1:
time: 153 us
  Pallas kernels  142 us (93%)
  local copies, waits for them, and re-layouts  9.38 us (6%)
    pallas_call x1, Pallas kernels, body(): pl.pallas_call(kernel, out_shape=(jax.ShapeDtypeStruct((rows, whole), bf1...  142 us
    unnamed x8, local copies, waits for them, and re-layouts  6.63 us

profile of v1, /device:TPU:1, one launch (start us, length us, event | category | flops | bytes accessed | tf_op | source)
XLA Modules:
  0.0 152.5 jit_solution(10334404405221024823)
XLA Ops:
  0.6 1.4 broadcast_in_dim.18.bkt
  2.0 1.4 broadcast_in_dim.19.sgn
  3.4 142.5 %gather_step_sketch.1 = (bf16[160,2048]{1,0:T(8,128)(2,1)}, bf16[160,6912]{1,0:T(8,128)(2,1)}, f32[160,512]{1,0:T(8,128)}, f32[160,512]{1,0:T(8,128)}) custom-call(bf16[128,6912]{1,0:T(8,128)(2,1)} %hid.1, bf16[160,2048]{1,0:T(8,128)(2,1)} %bitcast.14, bf16[160,2048]{1,0:T(8,128)(2,1)} %bitcast.15, bf16[160,6912]{1,0:T(8,128)(2,1)} %bitcast.13, ...), custom_call_target="tpu_custom_call" | custom-call | flops 12457082880 | bytes 6193152 | tf_op jit(solution)/shard_map/gather_step_sketch/pallas_call | solution.py:221
  145.9 2.0 %copy.16 = bf16[1,160,2048]{2,1,0:T(8,128)(2,1)} copy(bf16[1,160,2048]{2,1,0:T(8,128)(2,1)} %bitcast.10) | data formatting | bytes 1310720
  147.9 0.0 copy-start.1
  147.9 0.0 copy-start
  147.9 3.2 %copy.17 = bf16[1,160,6912]{2,1,0:T(8,128)(2,1)} copy(bf16[1,160,6912]{2,1,0:T(8,128)(2,1)} %bitcast.9) | data formatting | bytes 4423680
  151.1 0.0 copy-done.1
  151.1 0.7 copy.18
  151.8 0.0 copy-done
  151.8 0.7 copy.19
Async XLA Ops:
  147.9 3.2 %copy-start.1 = (f32[160,512]{1,0:T(8,128)S(1)}, f32[160,512]{1,0:T(8,128)}, u32[]{:S(2)}) copy-start(f32[160,512]{1,0:T(8,128)} %get-tuple-element.10) | copy-start | bytes 983044
  147.9 3.9 %copy-start = (f32[160,512]{1,0:T(8,128)S(1)}, f32[160,512]{1,0:T(8,128)}, u32[]{:S(2)}) copy-start(f32[160,512]{1,0:T(8,128)} %get-tuple-element.11) | copy-start | bytes 983044

commit v2 on v1

v2 whole, which is shorter than its diff:
```python
import jax
import jax.numpy as jnp
from jax import lax
from jax.experimental import pallas as pl
from jax.experimental.pallas import tpu as pltpu
from jax.sharding import PartitionSpec as P

MESH = pl.DeviceIdType.MESH
STEP_SIZE = 0.3
CONSENSUS = 0.5
CH = 256
LANES = 128
LEAD = 4
GAP = 3
PARTS = 3


def nt(a, b):
    return lax.dot_general(a, b, (((1,), (1,)), ((), ())), preferred_element_type=jnp.float32)


def nn(a, b):
    return jnp.dot(a, b, preferred_element_type=jnp.float32)


def chunk_row(ref, j):
    parts = CH // LANES
    return jnp.concatenate([ref[pl.ds(j * parts + p, 1), :] for p in range(parts)], axis=1)


def signed_table(bkt, sgn, j, sk):
    sign = (2 * chunk_row(sgn, j) - 1).astype(jnp.float32)
    hot = lax.broadcasted_iota(jnp.int32, (sk, CH), 0) == chunk_row(bkt, j)
    return sign, jnp.where(hot, jnp.broadcast_to(sign, (sk, CH)), 0.0).astype(jnp.bfloat16)


def gather_kernel(
    hid, res, cot, wgt, slf, bkt, sgn,
    out_s, out_st, out_sk, out_left, out_right,
    buf, wv, cv, rv, sv, sacc, stepped, lhs, kacc, skf, sk_send,
    lsem, insem, sem1, sem2, sem3, sibsem, ssem, xsem, osem,
):
    rows, ff = wgt.shape
    toks = hid.shape[0]
    nc = ff // CH
    nb, nf = lax.axis_size("blk"), lax.axis_size("fsdp")
    sk = slf.shape[1]
    blk, me = lax.axis_index("blk"), lax.axis_index("fsdp")
    xh, y, core = me // 8, (me // 2) % 4, me % 2
    xo = 1 - xh

    def at(a, b):
        return a * 8 + (b % 4) * 2 + core

    sibling = me + 1 - 2 * core
    up, down, across = at(xh, y + 1), at(xh, y + 3), at(xo, y)
    ahead, behind = (blk + 1) % nb, (blk + nb - 1) % nb

    def block(j, b):
        return buf.at[j, pl.ds(pl.multiple_of(b * toks, toks), toks), :]

    def columns(ref, j):
        return ref.at[:, pl.ds(pl.multiple_of(j * CH, CH), CH)]

    def load(j):
        return pltpu.make_async_copy(columns(hid, j), block(j, me), lsem.at[j])

    def send(j, b, to, recv, lane):
        pltpu.make_async_remote_copy(
            src_ref=block(j, b), dst_ref=block(j, b), send_sem=ssem.at[lane], recv_sem=recv.at[j],
            device_id=(blk, to), device_id_type=MESH,
        ).start()

    def arrived(j, sem, blocks):
        ref = buf.at[j, pl.ds(0, blocks * toks), :]
        pltpu.make_async_copy(ref, ref, sem.at[j]).wait()

    def own(j):
        load(j).wait()
        send(j, me, up, sem1, 0)
        send(j, me, down, sem1, 0)
        send(j, me, across, sem1, 0)
        send(j, me, sibling, sibsem, 1)

    def second(j):
        arrived(j, sem1, 3)
        kind = (j % 3) // 2
        turn = 1 + 2 * (j % 2)
        send(j, at(xh, y + 4 - turn), at(xh, y + turn), sem2, 0)
        send(j, (1 - kind) * across + kind * up, (1 - kind) * up + kind * across, sem2, 0)
        send(j, (1 - kind) * across + kind * down, (1 - kind) * down + kind * across, sem2, 0)
        send(j, up, sibling, sibsem, 1)
        send(j, down, sibling, sibsem, 1)
        send(j, across, sibling, sibsem, 1)

    def third(j):
        arrived(j, sem2, 3)
        kind = (j % 3) // 2
        turn = 1 + 2 * (1 - j % 2)
        send(
            j,
            (1 - kind) * at(xh, y + 2) + kind * at(xo, y + 4 - turn),
            (1 - kind) * across + kind * at(xh, y + turn),
            sem3,
            0,
        )
        send(j, at(xh, y + 2), sibling, sibsem, 1)
        send(j, at(xo, y + 1), sibling, sibsem, 1)
        send(j, at(xo, y + 3), sibling, sibsem, 1)

    def fourth(j):
        arrived(j, sem3, 1)
        send(j, at(xo, y + 2), sibling, sibsem, 1)

    def put_stepped(j):
        return pltpu.make_async_copy(stepped.at[j], out_st.at[j], osem.at[0])

    def gradient_part(j):
        arrived(j, sibsem, nf // 2)
        w = wv[:, pl.ds(pl.multiple_of(j * CH, CH), CH)]
        new = w.astype(jnp.float32) - (STEP_SIZE * ff**-0.5) * nn(cv[...], buf[j])
        stepped[j] = new
        put_stepped(j).start()
        sign, table = signed_table(bkt, sgn, j, sk)
        high = new.astype(jnp.bfloat16)
        lhs[pl.ds(0, rows), :] = high
        lhs[pl.ds(rows, rows), :] = (new - high.astype(jnp.float32)).astype(jnp.bfloat16)
        lhs[pl.ds(2 * rows, 16), :] = jnp.broadcast_to(sign, (16, CH)).astype(jnp.bfloat16)
        kacc[...] += nt(lhs[...], table)

    def product_part(j):
        sacc[...] += nt(wv[:, pl.ds(pl.multiple_of(j * CH, CH), CH)], buf[j])

    barrier = pltpu.get_barrier_semaphore()
    for to in (up, down, across, sibling):
        pl.semaphore_signal(barrier, inc=1, device_id=(blk, to), device_id_type=MESH)
    for to in (ahead, behind):
        pl.semaphore_signal(barrier, inc=1, device_id=(to, me), device_id_type=MESH)

    def start_load(j, c):
        load(j).start()
        return c

    lax.fori_loop(0, LEAD, start_load, 0)
    pl.semaphore_wait(barrier, 6)

    def lead(j, c):
        own(j)
        return c

    lax.fori_loop(0, LEAD, lead, 0)
    lax.fori_loop(LEAD, nc, start_load, 0)
    ins = [(cot, cv), (wgt, wv), (res, rv), (slf, sv)]
    ins = [pltpu.make_async_copy(a, b, insem.at[i]) for i, (a, b) in enumerate(ins)]
    for c in ins:
        c.start()
    sacc[...] = jnp.zeros_like(sacc)
    kacc[...] = jnp.zeros_like(kacc)
    for c in ins:
        c.wait()

    last = 2 * GAP + 1

    def step(i, c):
        @pl.when(i + LEAD < nc)
        def _():
            own(i + LEAD)

        @pl.when(i >= last)
        def _():
            gradient_part(i - last)

        @pl.when(i < nc)
        def _():
            second(i)

        @pl.when((i >= GAP) & (i < nc + GAP))
        def _():
            third(i - GAP)

        @pl.when((i >= 2 * GAP) & (i < nc + 2 * GAP))
        def _():
            fourth(i - 2 * GAP)

        @pl.when((i >= last) & (i < nc + last - 1))
        def _():
            product_part(i - last)

        return c

    lax.fori_loop(0, nc + last, step, 0)

    sketched = (sk / ff) * (
        kacc[pl.ds(0, rows), :] + kacc[pl.ds(rows, rows), :] - kacc[pl.ds(2 * rows, 1), :] * sv[...]
    )
    sk_send[...] = sketched.astype(jnp.bfloat16)
    swaps = [
        pltpu.make_async_remote_copy(
            src_ref=sk_send, dst_ref=dst, send_sem=xsem.at[2 * i], recv_sem=xsem.at[2 * i + 1],
            device_id=(to, me), device_id_type=MESH,
        )
        for i, (dst, to) in enumerate(((out_left, ahead), (out_right, behind)))
    ]
    for c in swaps:
        c.start()
    skf[...] = sketched
    outs = [pltpu.make_async_copy(skf, out_sk, osem.at[1])]
    outs[0].start()
    product_part(nc - 1)
    rv[...] = (rv[...].astype(jnp.float32) + (ff**-0.5) * sacc[...]).astype(jnp.bfloat16)
    outs.append(pltpu.make_async_copy(rv, out_s, osem.at[2]))
    outs[1].start()
    outs.append(pltpu.make_async_copy(stepped, out_st, osem.at[0]))
    for lane, blocks in ((0, 7), (1, 8)):
        ref = buf.at[:, pl.ds(0, blocks * toks), :]
        pltpu.make_async_copy(ref, ref, ssem.at[lane]).wait()
    for c in outs + swaps:
        c.wait()


def update_kernel(
    st, sketch, left, right, slf, mix, bkt, sgn, stream,
    out_s, out_w, out_self, out_mix,
    stv, wv, av, lv, rv, sv, mv, dv, tv, insem, stsem, osem,
):
    nc = st.shape[0]
    sk = slf.shape[1]
    part = nc // PARTS

    def columns(ref, p):
        return ref.at[:, pl.ds(pl.multiple_of(p * part * CH, CH), part * CH)]

    def get(p):
        there = pl.ds(p * part, part)
        return pltpu.make_async_copy(st.at[there], stv.at[there], stsem.at[p])

    ins = [(left, lv), (right, rv), (sketch, av), (mix, mv), (slf, sv), (stream, tv)]
    ins = [pltpu.make_async_copy(a, b, insem.at[i]) for i, (a, b) in enumerate(ins)]
    for c in ins:
        c.start()
    for p in range(PARTS):
        get(p).start()
    for c in ins[:5]:
        c.wait()
    new_self = sv[...] + av[...]
    new_mix = mv[...] + (lv[...].astype(jnp.float32) + av[...] + rv[...].astype(jnp.float32)) / 3.0
    dv[...] = (CONSENSUS * (new_mix - new_self)).astype(jnp.bfloat16)
    sv[...] = new_self
    mv[...] = new_mix
    ins[5].wait()
    outs = [(sv, out_self), (mv, out_mix), (tv, out_s)]
    outs = [pltpu.make_async_copy(a, b, osem.at[i]) for i, (a, b) in enumerate(outs)]
    for c in outs:
        c.start()

    def expand(p, c):
        get(p).wait()
        for q in range(part):
            j = p * part + q
            _, table = signed_table(bkt, sgn, j, sk)
            new = stv[j] + nn(dv[...], table)
            wv[:, pl.ds(pl.multiple_of(j * CH, CH), CH)] = new.astype(jnp.bfloat16)
        pltpu.make_async_copy(columns(wv, p), columns(out_w, p), osem.at[3]).start()
        return c

    lax.fori_loop(0, PARTS, expand, 0)
    outs.append(pltpu.make_async_copy(wv, out_w, osem.at[3]))
    for c in outs:
        c.wait()


def body(hidden, residual, cotangent, weight, self_sketch, mix_sketch, bucket, sign_bit):
    toks, ff = hidden.shape
    _, rows, whole = residual.shape
    sk = self_sketch.shape[2]
    nc = ff // CH
    f32, bf16 = jnp.float32, jnp.bfloat16
    anywhere = pl.BlockSpec(memory_space=pl.ANY)
    vmem = pl.BlockSpec(memory_space=pltpu.VMEM)
    dma = pltpu.SemaphoreType.DMA
    shape = jax.ShapeDtypeStruct
    bkt, sgn = bucket.reshape(-1, LANES), sign_bit.reshape(-1, LANES)
    stream, stepped, sketched, left, right = pl.pallas_call(
        gather_kernel,
        out_shape=(
            shape((rows, whole), bf16),
            shape((nc, rows, CH), f32),
            shape((rows, sk), f32),
            shape((rows, sk), bf16),
            shape((rows, sk), bf16),
        ),
        in_specs=[anywhere] * 5 + [vmem] * 2,
        out_specs=(anywhere,) * 5,
        scratch_shapes=[
            pltpu.VMEM((nc, whole, CH), bf16),
            pltpu.VMEM((rows, ff), bf16),
            pltpu.VMEM((rows, whole), bf16),
            pltpu.VMEM((rows, whole), bf16),
            pltpu.VMEM((rows, sk), f32),
            pltpu.VMEM((rows, whole), f32),
            pltpu.VMEM((nc, rows, CH), f32),
            pltpu.VMEM((2 * rows + 16, CH), bf16),
            pltpu.VMEM((2 * rows + 16, sk), f32),
            pltpu.VMEM((rows, sk), f32),
            pltpu.VMEM((rows, sk), bf16),
            dma((nc,)), dma((4,)), dma((nc,)), dma((nc,)), dma((nc,)), dma((nc,)), dma((2,)), dma((4,)), dma((3,)),
        ],
        compiler_params=pltpu.CompilerParams(
            collective_id=0, has_side_effects=True, vmem_limit_bytes=58 * 2**20
        ),
        cost_estimate=pl.CostEstimate(
            flops=2 * rows * ff * (2 * whole + 2 * sk), bytes_accessed=2 * (toks + 2 * rows) * ff, transcendentals=0
        ),
        name="gather_step_sketch",
    )(hidden, residual[0], cotangent[0], weight[0], self_sketch[0], bkt, sgn)
    outs = pl.pallas_call(
        update_kernel,
        out_shape=(
            shape((rows, whole), bf16),
            shape((rows, ff), bf16),
            shape((rows, sk), f32),
            shape((rows, sk), f32),
        ),
        in_specs=[anywhere] * 6 + [vmem] * 2 + [anywhere],
        out_specs=(anywhere,) * 4,
        scratch_shapes=[
            pltpu.VMEM((nc, rows, CH), f32),
            pltpu.VMEM((rows, ff), bf16),
            pltpu.VMEM((rows, sk), f32),
            pltpu.VMEM((rows, sk), bf16),
            pltpu.VMEM((rows, sk), bf16),
            pltpu.VMEM((rows, sk), f32),
            pltpu.VMEM((rows, sk), f32),
            pltpu.VMEM((rows, sk), bf16),
            pltpu.VMEM((rows, whole), bf16),
            dma((6,)), dma((PARTS,)), dma((4,)),
        ],
        compiler_params=pltpu.CompilerParams(vmem_limit_bytes=58 * 2**20),
        cost_estimate=pl.CostEstimate(
            flops=2 * rows * ff * sk, bytes_accessed=6 * rows * ff, transcendentals=0
        ),
        name="update",
    )(stepped, sketched, left, right, self_sketch[0], mix_sketch[0], bkt, sgn, stream)
    return tuple(o[None] for o in outs)


def solution(mesh):
    split = P("blk", "fsdp", None)
    return jax.shard_map(
        body,
        mesh=mesh,
        in_specs=(P(("blk", "fsdp"), None), split, split, split, split, split, P(), P()),
        out_specs=(split, split, split, split),
        check_vma=False,
    )
```

time: 153 us -> 124 us (0.81)
  Pallas kernels: 142 us -> 123 us
  local copies, waits for them, and re-layouts: 9.38 us -> 0 us
    pallas_call x1 -> x2, Pallas kernels: 142 us -> 123 us  [the longest x1 117 us: body(): pl.pallas_call(gather_kernel, out_shape=(shape((rows, whole), bf16), shap...]
    unnamed x8 -> x0, local copies, waits for them, and re-layouts: 6.63 us -> none
    broadcast_in_dim x2 -> x0, local copies, waits for them, and re-layouts: 2.75 us -> none  [the longest x1 1.38 us: body(): bucket[None]]
where the time goes in v2:
time: 124 us
  Pallas kernels  123 us (99%)
    pallas_call x1, Pallas kernels, body(): pl.pallas_call(gather_kernel, out_shape=(shape((rows, whole), bf16), shap...  117 us
    pallas_call x1, Pallas kernels, body(): pl.pallas_call(update_kernel, out_shape=(shape((rows, whole), bf16), shap...  6.38 us

profile of v2, /device:TPU:1, one launch (start us, length us, event | category | flops | bytes accessed | tf_op | source)
XLA Modules:
  0.0 124.1 jit_solution(1995650648920894430)
XLA Ops:
  0.6 117.1 %gather_step_sketch.1 = (bf16[160,2048]{1,0:T(8,128)(2,1)}, f32[27,160,256]{2,1,0:T(8,128)}, f32[160,512]{1,0:T(8,128)}, bf16[160,512]{1,0:T(8,128)(2,1)}, bf16[160,512]{1,0:T(8,128)(2,1)}) custom-call(bf16[128,6912]{1,0:T(8,128)(2,1)} %hid.1, bf16[160,2048]{1,0:T(8,128)(2,1)} %bitcast.20, bf16[160,2048]{1,0:T(8,128)(2,1)} %bitcast.21, ...), custom_call_target="tpu_custom_call" | custom-call | flops 11324620800 | bytes 6193152 | tf_op jit(solution)/shard_map/gather_step_sketch/pallas_call | solution.py:283
  117.7 6.4 %update.1 = (bf16[160,2048]{1,0:T(8,128)(2,1)}, bf16[160,6912]{1,0:T(8,128)(2,1)}, f32[160,512]{1,0:T(8,128)}, f32[160,512]{1,0:T(8,128)}) custom-call(f32[27,160,256]{2,1,0:T(8,128)} %get-tuple-element.13.st, f32[160,512]{1,0:T(8,128)} %get-tuple-element.14.sketch, bf16[160,512]{1,0:T(8,128)(2,1)} %get-tuple-element.15.left, ...), custom_call_target="tpu_custom_call" | custom-call | flops 1132462080 | bytes 6635520 | tf_op jit(solution)/shard_map/update/pallas_call | solution.py:316

commit v3 on v2

--- a/solution.py
+++ b/solution.py
@@ -11,7 +11,14 @@
 CH = 256
 LANES = 128
 LEAD = 4
-GAP = 3
+GAP = 2
+PAIRS = 8
+DEFER = 5
+AHEAD = 4
+FIRST_W = 2
+OTHER = 2
+LAG = 8
+PIECES = 5
 PARTS = 3
 
 
@@ -37,12 +44,13 @@
 def gather_kernel(
     hid, res, cot, wgt, slf, bkt, sgn,
     out_s, out_st, out_sk, out_left, out_right,
-    buf, wv, cv, rv, sv, sacc, stepped, lhs, kacc, skf, sk_send,
-    lsem, insem, sem1, sem2, sem3, sibsem, ssem, xsem, osem,
+    buf, wv, cv, rv, sv, sacc, stepped, lhs, kacc, skf, sk_send, wpart, gsend, grecv, psend, precv,
+    lsem, insem, sem1, sem2, sem3, sibsem, ssem, xsem, osem, gsem, wsem, psem,
 ):
     rows, ff = wgt.shape
     toks = hid.shape[0]
     nc = ff // CH
+    slots = nc - PAIRS
     nb, nf = lax.axis_size("blk"), lax.axis_size("fsdp")
     sk = slf.shape[1]
     blk, me = lax.axis_index("blk"), lax.axis_index("fsdp")
@@ -56,71 +64,81 @@
     up, down, across = at(xh, y + 1), at(xh, y + 3), at(xo, y)
     ahead, behind = (blk + 1) % nb, (blk + nb - 1) % nb
 
+    def chunk(i, half):
+        paired = (slots + PAIRS - 1 - i) // slots
+        return paired * (2 * i + half) + (1 - paired) * (i + PAIRS)
+
     def block(j, b):
         return buf.at[j, pl.ds(pl.multiple_of(b * toks, toks), toks), :]
 
-    def columns(ref, j):
-        return ref.at[:, pl.ds(pl.multiple_of(j * CH, CH), CH)]
+    def span(j):
+        return pl.ds(pl.multiple_of(j * CH, CH), CH)
 
     def load(j):
-        return pltpu.make_async_copy(columns(hid, j), block(j, me), lsem.at[j])
-
-    def send(j, b, to, recv, lane):
+        return pltpu.make_async_copy(hid.at[:, span(j)], block(j, me), lsem.at[j])
+
+    def send(i, j, b, to, recv, lane):
         pltpu.make_async_remote_copy(
-            src_ref=block(j, b), dst_ref=block(j, b), send_sem=ssem.at[lane], recv_sem=recv.at[j],
+            src_ref=block(j, b), dst_ref=block(j, b), send_sem=ssem.at[lane], recv_sem=recv.at[i],
             device_id=(blk, to), device_id_type=MESH,
         ).start()
 
-    def arrived(j, sem, blocks):
-        ref = buf.at[j, pl.ds(0, blocks * toks), :]
-        pltpu.make_async_copy(ref, ref, sem.at[j]).wait()
-
-    def own(j):
-        load(j).wait()
-        send(j, me, up, sem1, 0)
-        send(j, me, down, sem1, 0)
-        send(j, me, across, sem1, 0)
-        send(j, me, sibling, sibsem, 1)
-
-    def second(j):
-        arrived(j, sem1, 3)
-        kind = (j % 3) // 2
-        turn = 1 + 2 * (j % 2)
-        send(j, at(xh, y + 4 - turn), at(xh, y + turn), sem2, 0)
-        send(j, (1 - kind) * across + kind * up, (1 - kind) * up + kind * across, sem2, 0)
-        send(j, (1 - kind) * across + kind * down, (1 - kind) * down + kind * across, sem2, 0)
-        send(j, up, sibling, sibsem, 1)
-        send(j, down, sibling, sibsem, 1)
-        send(j, across, sibling, sibsem, 1)
-
-    def third(j):
-        arrived(j, sem2, 3)
-        kind = (j % 3) // 2
-        turn = 1 + 2 * (1 - j % 2)
-        send(
-            j,
-            (1 - kind) * at(xh, y + 2) + kind * at(xo, y + 4 - turn),
-            (1 - kind) * across + kind * at(xh, y + turn),
-            sem3,
-            0,
-        )
-        send(j, at(xh, y + 2), sibling, sibsem, 1)
-        send(j, at(xo, y + 1), sibling, sibsem, 1)
-        send(j, at(xo, y + 3), sibling, sibsem, 1)
-
-    def fourth(j):
-        arrived(j, sem3, 1)
-        send(j, at(xo, y + 2), sibling, sibsem, 1)
-
-    def put_stepped(j):
-        return pltpu.make_async_copy(stepped.at[j], out_st.at[j], osem.at[0])
-
-    def gradient_part(j):
-        arrived(j, sibsem, nf // 2)
-        w = wv[:, pl.ds(pl.multiple_of(j * CH, CH), CH)]
-        new = w.astype(jnp.float32) - (STEP_SIZE * ff**-0.5) * nn(cv[...], buf[j])
+    def hand(src, dst, recv, lane):
+        pltpu.make_async_remote_copy(
+            src_ref=src, dst_ref=dst, send_sem=ssem.at[lane], recv_sem=recv,
+            device_id=(blk, across), device_id_type=MESH,
+        ).start()
+
+    def landed(ref, sem):
+        pltpu.make_async_copy(ref, ref, sem).wait()
+
+    def arrived(i, sem, blocks):
+        landed(buf.at[i, pl.ds(0, blocks * toks), :], sem.at[i])
+
+    def cross(i):
+        other = chunk(i, xo)
+        load(other).wait()
+        send(i, other, me, across, sem1, 0)
+
+    def own(i):
+        j = chunk(i, xh)
+
+        @pl.when(i < PAIRS)
+        def _():
+            load(j).wait()
+
+        send(i, j, me, up, sem1, 0)
+        send(i, j, me, down, sem1, 0)
+        send(i, j, me, sibling, sibsem, 1)
+
+    def second(i):
+        arrived(i, sem1, 3)
+        j = chunk(i, xh)
+        turn = 1 + 2 * (i % 2)
+        send(i, j, at(xh, y + 4 - turn), at(xh, y + turn), sem2, 0)
+        send(i, j, across, up, sem2, 0)
+        send(i, j, across, down, sem2, 0)
+        send(i, j, up, sibling, sibsem, 1)
+        send(i, j, down, sibling, sibsem, 1)
+        send(i, j, across, sibling, sibsem, 1)
+
+    def third(i):
+        arrived(i, sem2, 3)
+        j = chunk(i, xh)
+        turn = 1 + 2 * (1 - i % 2)
+        send(i, j, at(xo, y + 4 - turn), at(xh, y + turn), sem3, 0)
+        send(i, j, at(xh, y + 2), sibling, sibsem, 1)
+        send(i, j, at(xo, y + 1), sibling, sibsem, 1)
+        send(i, j, at(xo, y + 3), sibling, sibsem, 1)
+
+    def fourth(i):
+        arrived(i, sem3, 1)
+        send(i, chunk(i, xh), at(xo, y + 2), sibling, sibsem, 1)
+
+    def finish(j, gradient):
+        new = wv[:, span(j)].astype(jnp.float32) - (STEP_SIZE * ff**-0.5) * gradient
         stepped[j] = new
-        put_stepped(j).start()
+        pltpu.make_async_copy(stepped.at[j], out_st.at[j], osem.at[0]).start()
         sign, table = signed_table(bkt, sgn, j, sk)
         high = new.astype(jnp.bfloat16)
         lhs[pl.ds(0, rows), :] = high
@@ -128,8 +146,31 @@
         lhs[pl.ds(2 * rows, 16), :] = jnp.broadcast_to(sign, (16, CH)).astype(jnp.bfloat16)
         kacc[...] += nt(lhs[...], table)
 
-    def product_part(j):
-        sacc[...] += nt(wv[:, pl.ds(pl.multiple_of(j * CH, CH), CH)], buf[j])
+    mine, theirs = pl.ds(0, rows), pl.ds(rows, rows)
+
+    def paired_step(k):
+        arrived(k, sibsem, nf // 2)
+        landed(wpart.at[k], wsem.at[k])
+        j = chunk(k, xh)
+        h = buf[j]
+        both = nn(cv[...], h)
+        gsend[k] = both[rows:].astype(jnp.bfloat16)
+        hand(gsend.at[k], grecv.at[k], gsem.at[k], 4)
+        finish(j, both[:rows])
+        sacc[...] += nt(jnp.concatenate([wv[:, span(j)], wpart[k]], axis=0), h)
+
+    def other_step(k):
+        landed(grecv.at[k], gsem.at[k])
+        finish(chunk(k, xo), grecv[k].astype(jnp.float32))
+
+    def gradient_part(i):
+        arrived(i, sibsem, nf // 2)
+        j = chunk(i, xh)
+        finish(j, nn(cv[mine, :], buf[j]))
+
+    def product_part(i):
+        j = chunk(i, xh)
+        sacc[mine, :] += nt(wv[:, span(j)], buf[j])
 
     barrier = pltpu.get_barrier_semaphore()
     for to in (up, down, across, sibling):
@@ -141,54 +182,97 @@
         load(j).start()
         return c
 
-    lax.fori_loop(0, LEAD, start_load, 0)
+    lax.fori_loop(0, 2 * AHEAD, start_load, 0)
+    ins = [(cot, cv.at[mine, :]), (wgt, wv), (res, rv), (slf, sv)]
+    ins = [pltpu.make_async_copy(a, b, insem.at[i]) for i, (a, b) in enumerate(ins)]
+    ins[0].start()
     pl.semaphore_wait(barrier, 6)
 
-    def lead(j, c):
-        own(j)
+    def lead(i, c):
+        cross(i)
+        own(i)
+        return c
+
+    def lead_cross(i, c):
+        cross(i)
         return c
 
     lax.fori_loop(0, LEAD, lead, 0)
-    lax.fori_loop(LEAD, nc, start_load, 0)
-    ins = [(cot, cv), (wgt, wv), (res, rv), (slf, sv)]
-    ins = [pltpu.make_async_copy(a, b, insem.at[i]) for i, (a, b) in enumerate(ins)]
-    for c in ins:
+    for c in ins[1:]:
         c.start()
+    lax.fori_loop(2 * AHEAD, nc, start_load, 0)
+    lax.fori_loop(LEAD, AHEAD, lead_cross, 0)
     sacc[...] = jnp.zeros_like(sacc)
     kacc[...] = jnp.zeros_like(kacc)
     for c in ins:
         c.wait()
 
     last = 2 * GAP + 1
+    strip = rows // PIECES
+    first_sum = LAG + PAIRS
 
     def step(i, c):
-        @pl.when(i + LEAD < nc)
+        @pl.when(i + AHEAD < slots)
+        def _():
+            cross(i + AHEAD)
+
+        @pl.when(i + LEAD < slots)
         def _():
             own(i + LEAD)
 
-        @pl.when(i >= last)
+        @pl.when(i == 0)
+        def _():
+            for p in range(PIECES):
+                hand(cv.at[pl.ds(p * strip, strip), :], cv.at[pl.ds(rows + p * strip, strip), :], psem.at[0], 2)
+
+        @pl.when((i >= FIRST_W) & (i < FIRST_W + PAIRS // 2))
+        def _():
+            for q in range(2):
+                k = 2 * (i - FIRST_W) + q
+                hand(wv.at[:, span(chunk(k, xo))], wpart.at[k], wsem.at[k], 3)
+
+        @pl.when((i >= first_sum) & (i < first_sum + PIECES))
+        def _():
+            at_row = pl.multiple_of((i - first_sum) * strip, strip)
+            there = pl.ds(at_row, strip)
+            psend[there, :] = sacc[pl.ds(rows + at_row, strip), :].astype(jnp.bfloat16)
+            hand(psend.at[there, :], precv.at[there, :], psem.at[1], 5)
+
+        @pl.when(i < slots)
+        def _():
+            second(i)
+
+        @pl.when((i >= GAP) & (i < slots + GAP))
+        def _():
+            third(i - GAP)
+
+        @pl.when((i >= 2 * GAP) & (i < slots + 2 * GAP))
+        def _():
+            fourth(i - 2 * GAP)
+
+        @pl.when(i >= PAIRS + last)
         def _():
             gradient_part(i - last)
 
-        @pl.when(i < nc)
-        def _():
-            second(i)
-
-        @pl.when((i >= GAP) & (i < nc + GAP))
-        def _():
-            third(i - GAP)
-
-        @pl.when((i >= 2 * GAP) & (i < nc + 2 * GAP))
-        def _():
-            fourth(i - 2 * GAP)
-
-        @pl.when((i >= last) & (i < nc + last - 1))
-        def _():
-            product_part(i - last)
-
-        return c
-
-    lax.fori_loop(0, nc + last, step, 0)
+        @pl.when(i == LAG)
+        def _():
+            landed(cv.at[theirs, :], psem.at[0])
+
+        @pl.when((i >= LAG) & (i < first_sum))
+        def _():
+            paired_step(i - LAG)
+
+        @pl.when((i >= (LAG + OTHER)) & (i < (LAG + OTHER) + PAIRS))
+        def _():
+            other_step(i - (LAG + OTHER))
+
+        @pl.when(i >= PAIRS + last + DEFER)
+        def _():
+            product_part(i - last - DEFER)
+
+        return c
+
+    lax.fori_loop(0, slots + last, step, 0)
 
     sketched = (sk / ff) * (
         kacc[pl.ds(0, rows), :] + kacc[pl.ds(rows, rows), :] - kacc[pl.ds(2 * rows, 1), :] * sv[...]
@@ -206,14 +290,22 @@
     skf[...] = sketched
     outs = [pltpu.make_async_copy(skf, out_sk, osem.at[1])]
     outs[0].start()
-    product_part(nc - 1)
-    rv[...] = (rv[...].astype(jnp.float32) + (ff**-0.5) * sacc[...]).astype(jnp.bfloat16)
+
+    def product_left(i, c):
+        product_part(i)
+        return c
+
+    lax.fori_loop(slots - DEFER, slots, product_left, 0)
+    landed(precv, psem.at[1])
+    total = sacc[mine, :] + precv[...].astype(jnp.float32)
+    rv[...] = (rv[...].astype(jnp.float32) + (ff**-0.5) * total).astype(jnp.bfloat16)
     outs.append(pltpu.make_async_copy(rv, out_s, osem.at[2]))
     outs[1].start()
     outs.append(pltpu.make_async_copy(stepped, out_st, osem.at[0]))
     for lane, blocks in ((0, 7), (1, 8)):
-        ref = buf.at[:, pl.ds(0, blocks * toks), :]
-        pltpu.make_async_copy(ref, ref, ssem.at[lane]).wait()
+        landed(buf.at[pl.ds(0, slots), pl.ds(0, blocks * toks), :], ssem.at[lane])
+    for i, ref in enumerate((cv.at[theirs, :], wpart, gsend, precv)):
+        landed(ref, ssem.at[2 + i])
     for c in outs + swaps:
         c.wait()
 
@@ -294,16 +386,22 @@
         scratch_shapes=[
             pltpu.VMEM((nc, whole, CH), bf16),
             pltpu.VMEM((rows, ff), bf16),
-            pltpu.VMEM((rows, whole), bf16),
+            pltpu.VMEM((2 * rows, whole), bf16),
             pltpu.VMEM((rows, whole), bf16),
             pltpu.VMEM((rows, sk), f32),
-            pltpu.VMEM((rows, whole), f32),
+            pltpu.VMEM((2 * rows, whole), f32),
             pltpu.VMEM((nc, rows, CH), f32),
             pltpu.VMEM((2 * rows + 16, CH), bf16),
             pltpu.VMEM((2 * rows + 16, sk), f32),
             pltpu.VMEM((rows, sk), f32),
             pltpu.VMEM((rows, sk), bf16),
-            dma((nc,)), dma((4,)), dma((nc,)), dma((nc,)), dma((nc,)), dma((nc,)), dma((2,)), dma((4,)), dma((3,)),
+            pltpu.VMEM((PAIRS, rows, CH), bf16),
+            pltpu.VMEM((PAIRS, rows, CH), bf16),
+            pltpu.VMEM((PAIRS, rows, CH), bf16),
+            pltpu.VMEM((rows, whole), bf16),
+            pltpu.VMEM((rows, whole), bf16),
+            dma((nc,)), dma((4,)), dma((nc,)), dma((nc,)), dma((nc,)), dma((nc,)), dma((6,)), dma((4,)), dma((3,)),
+            dma((PAIRS,)), dma((PAIRS,)), dma((2,)),
         ],
         compiler_params=pltpu.CompilerParams(
             collective_id=0, has_side_effects=True, vmem_limit_bytes=58 * 2**20

time: 124 us -> 112 us (0.903)
  Pallas kernels: 123 us -> 111 us
    pallas_call x1, Pallas kernels: 117 us -> 105 us  [body(): pl.pallas_call(gather_kernel, out_shape=(shape((rows, whole), bf16), shap...]
where the time goes in v3:
time: 112 us
  Pallas kernels  111 us (99%)
    pallas_call x1, Pallas kernels, body(): pl.pallas_call(gather_kernel, out_shape=(shape((rows, whole), bf16), shap...  105 us
    pallas_call x1, Pallas kernels, body(): pl.pallas_call(update_kernel, out_shape=(shape((rows, whole), bf16), shap...  6.36 us

profile of v3, /device:TPU:1, one launch (start us, length us, event | category | flops | bytes accessed | tf_op | source)
XLA Modules:
  0.0 111.6 jit_solution(17711329195444129273)
XLA Ops:
  0.6 104.6 %gather_step_sketch.1 = (bf16[160,2048]{1,0:T(8,128)(2,1)}, f32[27,160,256]{2,1,0:T(8,128)}, f32[160,512]{1,0:T(8,128)}, bf16[160,512]{1,0:T(8,128)(2,1)}, bf16[160,512]{1,0:T(8,128)(2,1)}) custom-call(bf16[128,6912]{1,0:T(8,128)(2,1)} %hid.1, bf16[160,2048]{1,0:T(8,128)(2,1)} %bitcast.20, bf16[160,2048]{1,0:T(8,128)(2,1)} %bitcast.21, ...), custom_call_target="tpu_custom_call" | custom-call | flops 11324620800 | bytes 6193152 | tf_op jit(solution)/shard_map/gather_step_sketch/pallas_call | solution.py:375
  105.2 6.4 %update.1 = (bf16[160,2048]{1,0:T(8,128)(2,1)}, bf16[160,6912]{1,0:T(8,128)(2,1)}, f32[160,512]{1,0:T(8,128)}, f32[160,512]{1,0:T(8,128)}) custom-call(f32[27,160,256]{2,1,0:T(8,128)} %get-tuple-element.13.st, f32[160,512]{1,0:T(8,128)} %get-tuple-element.14.sketch, bf16[160,512]{1,0:T(8,128)(2,1)} %get-tuple-element.15.left, ...), custom_call_target="tpu_custom_call" | custom-call | flops 1132462080 | bytes 6635520 | tf_op jit(solution)/shard_map/update/pallas_call | solution.py:414

commit v4 on v3

--- a/solution.py
+++ b/solution.py
@@ -20,6 +20,7 @@
 LAG = 8
 PIECES = 5
 PARTS = 3
+PUT = 3
 
 
 def nt(a, b):
@@ -42,9 +43,9 @@
 
 
 def gather_kernel(
-    hid, res, cot, wgt, slf, bkt, sgn,
+    hid, res, cot, wgt, slf, bucket, bits,
     out_s, out_st, out_sk, out_left, out_right,
-    buf, wv, cv, rv, sv, sacc, stepped, lhs, kacc, skf, sk_send, wpart, gsend, grecv, psend, precv,
+    buf, wv, cv, rv, sv, sacc, stepped, lhs, kacc, skf, sk_send, wpart, gsend, grecv, psend, precv, bkt, sgn,
     lsem, insem, sem1, sem2, sem3, sibsem, ssem, xsem, osem, gsem, wsem, psem,
 ):
     rows, ff = wgt.shape
@@ -183,7 +184,7 @@
         return c
 
     lax.fori_loop(0, 2 * AHEAD, start_load, 0)
-    ins = [(cot, cv.at[mine, :]), (wgt, wv), (res, rv), (slf, sv)]
+    ins = [(cot, cv.at[mine, :]), (wgt, wv), (bucket, bkt), (bits, sgn), (slf, sv), (res, rv)]
     ins = [pltpu.make_async_copy(a, b, insem.at[i]) for i, (a, b) in enumerate(ins)]
     ins[0].start()
     pl.semaphore_wait(barrier, 6)
@@ -231,12 +232,12 @@
                 k = 2 * (i - FIRST_W) + q
                 hand(wv.at[:, span(chunk(k, xo))], wpart.at[k], wsem.at[k], 3)
 
-        @pl.when((i >= first_sum) & (i < first_sum + PIECES))
-        def _():
-            at_row = pl.multiple_of((i - first_sum) * strip, strip)
-            there = pl.ds(at_row, strip)
-            psend[there, :] = sacc[pl.ds(rows + at_row, strip), :].astype(jnp.bfloat16)
-            hand(psend.at[there, :], precv.at[there, :], psem.at[1], 5)
+        @pl.when(i == first_sum)
+        def _():
+            psend[...] = sacc[theirs, :].astype(jnp.bfloat16)
+            for p in range(PIECES):
+                there = pl.ds(p * strip, strip)
+                hand(psend.at[there, :], precv.at[there, :], psem.at[1], 5)
 
         @pl.when(i < slots)
         def _():
@@ -311,35 +312,35 @@
 
 
 def update_kernel(
-    st, sketch, left, right, slf, mix, bkt, sgn, stream,
+    st, sketch, left, right, slf, mix, bucket, bits, stream,
     out_s, out_w, out_self, out_mix,
-    stv, wv, av, lv, rv, sv, mv, dv, tv, insem, stsem, osem,
+    stv, wv, av, lv, rv, sv, mv, dv, tv, bkt, sgn, insem, stsem, osem,
 ):
     nc = st.shape[0]
     sk = slf.shape[1]
     part = nc // PARTS
 
-    def columns(ref, p):
-        return ref.at[:, pl.ds(pl.multiple_of(p * part * CH, CH), part * CH)]
+    def columns(ref, j):
+        return ref.at[:, pl.ds(pl.multiple_of(j * CH, CH), PUT * CH)]
 
     def get(p):
         there = pl.ds(p * part, part)
         return pltpu.make_async_copy(st.at[there], stv.at[there], stsem.at[p])
 
-    ins = [(left, lv), (right, rv), (sketch, av), (mix, mv), (slf, sv), (stream, tv)]
+    ins = [(left, lv), (right, rv), (sketch, av), (mix, mv), (slf, sv), (bucket, bkt), (bits, sgn), (stream, tv)]
     ins = [pltpu.make_async_copy(a, b, insem.at[i]) for i, (a, b) in enumerate(ins)]
     for c in ins:
         c.start()
     for p in range(PARTS):
         get(p).start()
-    for c in ins[:5]:
+    for c in ins[:7]:
         c.wait()
     new_self = sv[...] + av[...]
     new_mix = mv[...] + (lv[...].astype(jnp.float32) + av[...] + rv[...].astype(jnp.float32)) / 3.0
     dv[...] = (CONSENSUS * (new_mix - new_self)).astype(jnp.bfloat16)
     sv[...] = new_self
     mv[...] = new_mix
-    ins[5].wait()
+    ins[7].wait()
     outs = [(sv, out_self), (mv, out_mix), (tv, out_s)]
     outs = [pltpu.make_async_copy(a, b, osem.at[i]) for i, (a, b) in enumerate(outs)]
     for c in outs:
@@ -352,7 +353,9 @@
             _, table = signed_table(bkt, sgn, j, sk)
             new = stv[j] + nn(dv[...], table)
             wv[:, pl.ds(pl.multiple_of(j * CH, CH), CH)] = new.astype(jnp.bfloat16)
-        pltpu.make_async_copy(columns(wv, p), columns(out_w, p), osem.at[3]).start()
+            if q % PUT == PUT - 1:
+                there = j - PUT + 1
+                pltpu.make_async_copy(columns(wv, there), columns(out_w, there), osem.at[3]).start()
         return c
 
     lax.fori_loop(0, PARTS, expand, 0)
@@ -368,7 +371,6 @@
     nc = ff // CH
     f32, bf16 = jnp.float32, jnp.bfloat16
     anywhere = pl.BlockSpec(memory_space=pl.ANY)
-    vmem = pl.BlockSpec(memory_space=pltpu.VMEM)
     dma = pltpu.SemaphoreType.DMA
     shape = jax.ShapeDtypeStruct
     bkt, sgn = bucket.reshape(-1, LANES), sign_bit.reshape(-1, LANES)
@@ -381,7 +383,7 @@
             shape((rows, sk), bf16),
             shape((rows, sk), bf16),
         ),
-        in_specs=[anywhere] * 5 + [vmem] * 2,
+        in_specs=[anywhere] * 7,
         out_specs=(anywhere,) * 5,
         scratch_shapes=[
             pltpu.VMEM((nc, whole, CH), bf16),
@@ -400,7 +402,9 @@
             pltpu.VMEM((PAIRS, rows, CH), bf16),
             pltpu.VMEM((rows, whole), bf16),
             pltpu.VMEM((rows, whole), bf16),
-            dma((nc,)), dma((4,)), dma((nc,)), dma((nc,)), dma((nc,)), dma((nc,)), dma((6,)), dma((4,)), dma((3,)),
+            pltpu.VMEM(bkt.shape, jnp.int32),
+            pltpu.VMEM(bkt.shape, jnp.int32),
+            dma((nc,)), dma((6,)), dma((nc,)), dma((nc,)), dma((nc,)), dma((nc,)), dma((6,)), dma((4,)), dma((3,)),
             dma((PAIRS,)), dma((PAIRS,)), dma((2,)),
         ],
         compiler_params=pltpu.CompilerParams(
@@ -419,7 +423,7 @@
             shape((rows, sk), f32),
             shape((rows, sk), f32),
         ),
-        in_specs=[anywhere] * 6 + [vmem] * 2 + [anywhere],
+        in_specs=[anywhere] * 9,
         out_specs=(anywhere,) * 4,
         scratch_shapes=[
             pltpu.VMEM((nc, rows, CH), f32),
@@ -431,7 +435,9 @@
             pltpu.VMEM((rows, sk), f32),
             pltpu.VMEM((rows, sk), bf16),
             pltpu.VMEM((rows, whole), bf16),
-            dma((6,)), dma((PARTS,)), dma((4,)),
+            pltpu.VMEM(bkt.shape, jnp.int32),
+            pltpu.VMEM(bkt.shape, jnp.int32),
+            dma((8,)), dma((PARTS,)), dma((4,)),
         ],
         compiler_params=pltpu.CompilerParams(vmem_limit_bytes=58 * 2**20),
         cost_estimate=pl.CostEstimate(

time: 112 us -> 110 us (0.982)
  Pallas kernels: 111 us -> 109 us
where the time goes in v4:
time: 110 us
  Pallas kernels  109 us (99%)
    pallas_call x1, Pallas kernels, body(): pl.pallas_call(gather_kernel, out_shape=(shape((rows, whole), bf16), shap...  104 us
    pallas_call x1, Pallas kernels, body(): pl.pallas_call(update_kernel, out_shape=(shape((rows, whole), bf16), shap...  5.48 us

profile of v4, /device:TPU:1, one launch (start us, length us, event | category | flops | bytes accessed | tf_op | source)
XLA Modules:
  0.0 110.0 jit_solution(2048790985229752390)
XLA Ops:
  0.6 103.9 %gather_step_sketch.1 = (bf16[160,2048]{1,0:T(8,128)(2,1)}, f32[27,160,256]{2,1,0:T(8,128)}, f32[160,512]{1,0:T(8,128)}, bf16[160,512]{1,0:T(8,128)(2,1)}, bf16[160,512]{1,0:T(8,128)(2,1)}) custom-call(bf16[128,6912]{1,0:T(8,128)(2,1)} %hid.1, bf16[160,2048]{1,0:T(8,128)(2,1)} %bitcast.20, bf16[160,2048]{1,0:T(8,128)(2,1)} %bitcast.21, ...), custom_call_target="tpu_custom_call" | custom-call | flops 11324620800 | bytes 6193152 | tf_op jit(solution)/shard_map/gather_step_sketch/pallas_call | solution.py:377
  104.5 5.5 %update.1 = (bf16[160,2048]{1,0:T(8,128)(2,1)}, bf16[160,6912]{1,0:T(8,128)(2,1)}, f32[160,512]{1,0:T(8,128)}, f32[160,512]{1,0:T(8,128)}) custom-call(f32[27,160,256]{2,1,0:T(8,128)} %get-tuple-element.13.st, f32[160,512]{1,0:T(8,128)} %get-tuple-element.14.sketch, bf16[160,512]{1,0:T(8,128)(2,1)} %get-tuple-element.15.left, ...), custom_call_target="tpu_custom_call" | custom-call | flops 1132462080 | bytes 6635520 | tf_op jit(solution)/shard_map/update/pallas_call | solution.py:418

commit v5 on v4

--- a/solution.py
+++ b/solution.py
@@ -13,10 +13,10 @@
 LEAD = 4
 GAP = 2
 PAIRS = 8
-DEFER = 5
+DEFER = 1
 AHEAD = 4
 FIRST_W = 2
-OTHER = 2
+OTHER = 4
 LAG = 8
 PIECES = 5
 PARTS = 3
@@ -112,11 +112,19 @@
         send(i, j, me, down, sem1, 0)
         send(i, j, me, sibling, sibsem, 1)
 
+    def forward(i, j, a, recv):
+        half = toks // 2
+        for b, to, start in ((at(a, y + 3), up, 0), (at(a, y + 1), down, half)):
+            ref = buf.at[j, pl.ds(pl.multiple_of(b * toks + start, half), half), :]
+            pltpu.make_async_remote_copy(
+                src_ref=ref, dst_ref=ref, send_sem=ssem.at[0], recv_sem=recv.at[i],
+                device_id=(blk, to), device_id_type=MESH,
+            ).start()
+
     def second(i):
         arrived(i, sem1, 3)
         j = chunk(i, xh)
-        turn = 1 + 2 * (i % 2)
-        send(i, j, at(xh, y + 4 - turn), at(xh, y + turn), sem2, 0)
+        forward(i, j, xh, sem2)
         send(i, j, across, up, sem2, 0)
         send(i, j, across, down, sem2, 0)
         send(i, j, up, sibling, sibsem, 1)
@@ -126,8 +134,7 @@
     def third(i):
         arrived(i, sem2, 3)
         j = chunk(i, xh)
-        turn = 1 + 2 * (1 - i % 2)
-        send(i, j, at(xo, y + 4 - turn), at(xh, y + turn), sem3, 0)
+        forward(i, j, xo, sem3)
         send(i, j, at(xh, y + 2), sibling, sibsem, 1)
         send(i, j, at(xo, y + 1), sibling, sibsem, 1)
         send(i, j, at(xo, y + 3), sibling, sibsem, 1)

time: 110 us -> 109 us (level)
  no operation moved by 1% of the time
where the time goes in v5:
time: 109 us
  Pallas kernels  109 us (100%)
    pallas_call x1, Pallas kernels, body(): pl.pallas_call(gather_kernel, out_shape=(shape((rows, whole), bf16), shap...  103 us
    pallas_call x1, Pallas kernels, body(): pl.pallas_call(update_kernel, out_shape=(shape((rows, whole), bf16), shap...  5.47 us

profile of v5, /device:TPU:1, one launch (start us, length us, event | category | flops | bytes accessed | tf_op | source)
XLA Modules:
  0.0 109.3 jit_solution(18250529660745779383)
XLA Ops:
  0.6 103.2 %gather_step_sketch.1 = (bf16[160,2048]{1,0:T(8,128)(2,1)}, f32[27,160,256]{2,1,0:T(8,128)}, f32[160,512]{1,0:T(8,128)}, bf16[160,512]{1,0:T(8,128)(2,1)}, bf16[160,512]{1,0:T(8,128)(2,1)}) custom-call(bf16[128,6912]{1,0:T(8,128)(2,1)} %hid.1, bf16[160,2048]{1,0:T(8,128)(2,1)} %bitcast.20, bf16[160,2048]{1,0:T(8,128)(2,1)} %bitcast.21, ...), custom_call_target="tpu_custom_call" | custom-call | flops 11324620800 | bytes 6193152 | tf_op jit(solution)/shard_map/gather_step_sketch/pallas_call | solution.py:384
  103.9 5.5 %update.1 = (bf16[160,2048]{1,0:T(8,128)(2,1)}, bf16[160,6912]{1,0:T(8,128)(2,1)}, f32[160,512]{1,0:T(8,128)}, f32[160,512]{1,0:T(8,128)}) custom-call(f32[27,160,256]{2,1,0:T(8,128)} %get-tuple-element.13.st, f32[160,512]{1,0:T(8,128)} %get-tuple-element.14.sketch, bf16[160,512]{1,0:T(8,128)(2,1)} %get-tuple-element.15.left, ...), custom_call_target="tpu_custom_call" | custom-call | flops 1132462080 | bytes 6635520 | tf_op jit(solution)/shard_map/update/pallas_call | solution.py:425
